TPU v7x, 128 devices: a whole 4x4x4 slice. The times are simulated.
128 devices in a mesh: dp: 2 (over z_hi), expert: 64 (over x, y, z_lo, core).
Axes of the slice: x: 4, y: 4, z: 4 (z_hi: 2, z_lo: 2; z = z_hi * 2 + z_lo), core: 2. Of those that a mesh axis runs over, the one named last changes fastest.
Arguments:
- tokens: bfloat16 [8192, 2048], P('expert'), may hold values from -6 to 6
- routing: int32 [8192, 8], P('expert'), may hold values from 0 to 127, all different within a row; in each aligned block of 128 rows (0 to 127, 128 to 255, ...) at most 12 rows name the same one
- route_gates: float32 [8192, 8], P('expert'), may hold values from 0.03 to 0.3
- gate_weight: bfloat16 [128, 2048, 768], P('expert', None, 'dp'), may hold values from -0.125 to 0.125
- up_weight: bfloat16 [128, 2048, 768], P('expert', None, 'dp'), may hold values from -0.125 to 0.125
- down_weight: bfloat16 [128, 2048, 768], P('expert', None, 'dp'), may hold values from -0.21875 to 0.21875
- cotangent: bfloat16 [8192, 2048], P('expert'), may hold values from -4 to 4
Outputs:
- mixed: bfloat16 [8192, 2048], P('expert', 'dp')
- token_grad: bfloat16 [8192, 2048], P('expert', 'dp')
- gates_grad: float32 [8192, 8], P('expert')
- gate_grad: bfloat16 [128, 2048, 768], P('expert', None, 'dp')
- up_grad: bfloat16 [128, 2048, 768], P('expert', None, 'dp')
- down_grad: bfloat16 [128, 2048, 768], P('expert', None, 'dp')
Inputs may be any that keep to these rules, and one draw needn't show every extreme that they name: `routing`: each row names 8 different experts. Among the rows of one index of expert (aligned blocks of 128 rows) no expert is named more than 12 times, a bound that some block reaches.
All inputs are finite; a program needn't handle non-finite values.
Results may differ from a plain program's by a relative error of at most 0.012.
Values may be sent and summed in bfloat16 or wider, within the bound.
No kernel may reach another device: no remote copies, remote signals or barrier semaphores. Data moves between devices by JAX's collectives and lax.ppermute only.
A program may use at most 192 MiB of HBM per device.

v0:
```python
import jax
import jax.numpy as jnp
from jax import lax
from jax.sharding import PartitionSpec as P


def expert_forward(slot_rows, w_gate, w_up, w_down):
    gate_pre = jnp.einsum("jrd,jdf->jrf", slot_rows, w_gate, preferred_element_type=jnp.float32)
    up_pre = jnp.einsum("jrd,jdf->jrf", slot_rows, w_up, preferred_element_type=jnp.float32)
    sigmoid_gate = jax.nn.sigmoid(gate_pre)
    active = gate_pre * sigmoid_gate
    hidden = (active * up_pre).astype(jnp.bfloat16)
    out_part = jnp.einsum("jrf,jdf->jrd", hidden, w_down, preferred_element_type=jnp.float32)
    return (out_part, (gate_pre, up_pre, sigmoid_gate, active, hidden))


def expert_backward(slot_rows, slot_back, saved, w_gate, w_up, w_down):
    gate_pre, up_pre, sigmoid_gate, active, hidden = saved
    dhidden = jnp.einsum("jrd,jdf->jrf", slot_back, w_down, preferred_element_type=jnp.float32)
    d_gate = (dhidden * up_pre * sigmoid_gate * (1.0 + gate_pre * (1.0 - sigmoid_gate))).astype(
        jnp.bfloat16
    )
    d_up = (dhidden * active).astype(jnp.bfloat16)
    row_part = jnp.einsum("jrf,jdf->jrd", d_gate, w_gate, preferred_element_type=jnp.float32)
    row_part = row_part + jnp.einsum("jrf,jdf->jrd", d_up, w_up, preferred_element_type=jnp.float32)
    grad_g = jnp.einsum("jrd,jrf->jdf", slot_rows, d_gate, preferred_element_type=jnp.float32)
    grad_u = jnp.einsum("jrd,jrf->jdf", slot_rows, d_up, preferred_element_type=jnp.float32)
    grad_d = jnp.einsum("jrd,jrf->jdf", slot_back, hidden, preferred_element_type=jnp.float32)
    return (row_part, (grad_g, grad_u, grad_d))


def body(tokens, routing, route_gates, gate_weight, up_weight, down_weight, cotangent):
    rows_here, width = tokens.shape
    picks = routing.shape[1]
    local_count = gate_weight.shape[0]
    devices = lax.axis_size("expert")
    experts_all = local_count * devices
    capacity = 3 * rows_here * picks // (2 * experts_all)
    half_width = width // lax.axis_size("dp")
    member = lax.axis_index("dp")
    offset = member * half_width
    cot_half = lax.dynamic_slice_in_dim(cotangent, offset, half_width, 1)
    chosen = routing.reshape(-1)
    one_hot = (chosen[:, None] == jnp.arange(experts_all, dtype=jnp.int32)[None, :]).astype(
        jnp.int32
    )
    running = jnp.cumsum(one_hot, axis=0) - one_hot
    within = jnp.sum(running * one_hot, axis=1)
    owners = chosen // local_count
    slots = chosen % local_count
    source_row = jnp.arange(rows_here * picks, dtype=jnp.int32) // picks
    flat_gates = route_gates.reshape(-1)
    x_rows = tokens[source_row]
    weighted = (flat_gates[:, None] * cotangent[source_row].astype(jnp.float32)).astype(
        jnp.bfloat16
    )

    def scatter_rows(values):
        buffer = jnp.zeros((local_count, devices, capacity) + values.shape[1:], values.dtype)
        return buffer.at[slots, owners, within].set(values)

    def gather_rows(buffer):
        return buffer[slots, owners, within]

    short_shape = (local_count, devices, capacity, half_width)
    got_rows = lax.all_to_all(
        scatter_rows(x_rows), "expert", split_axis=1, concat_axis=1, tiled=True
    )
    slot_rows = got_rows.reshape(local_count, devices * capacity, width)
    out_part, saved = expert_forward(slot_rows, gate_weight, up_weight, down_weight)
    out_sum = lax.psum_scatter(out_part, "dp", scatter_dimension=2, tiled=True)
    back_out = lax.all_to_all(
        out_sum.astype(jnp.bfloat16).reshape(short_shape),
        "expert",
        split_axis=1,
        concat_axis=1,
        tiled=True,
    )
    got_back = lax.all_to_all(
        scatter_rows(weighted), "expert", split_axis=1, concat_axis=1, tiled=True
    )
    slot_back = got_back.reshape(local_count, devices * capacity, width)
    row_part, weight_grads = expert_backward(
        slot_rows, slot_back, saved, gate_weight, up_weight, down_weight
    )
    row_sum = lax.psum_scatter(row_part, "dp", scatter_dimension=2, tiled=True)
    back_grad = lax.all_to_all(
        row_sum.astype(jnp.bfloat16).reshape(short_shape),
        "expert",
        split_axis=1,
        concat_axis=1,
        tiled=True,
    )
    expert_rows = gather_rows(back_out).reshape(rows_here, picks, half_width)
    gate_part = jnp.einsum("td,tkd->tk", cot_half, expert_rows, preferred_element_type=jnp.float32)
    mixed = jnp.einsum("tk,tkd->td", route_gates, expert_rows.astype(jnp.float32)).astype(
        jnp.bfloat16
    )
    grad_rows = gather_rows(back_grad).reshape(rows_here, picks, half_width)
    token_grad = jnp.sum(grad_rows.astype(jnp.float32), axis=1).astype(jnp.bfloat16)
    grad_g = weight_grads[0].astype(jnp.bfloat16)
    grad_u = weight_grads[1].astype(jnp.bfloat16)
    grad_d = weight_grads[2].astype(jnp.bfloat16)
    gates_grad = lax.psum(gate_part, "dp")
    return (mixed, token_grad, gates_grad, grad_g, grad_u, grad_d)


def solution(mesh):
    in_specs = (
        P("expert", None),
        P("expert", None),
        P("expert", None),
        P("expert", None, "dp"),
        P("expert", None, "dp"),
        P("expert", None, "dp"),
        P("expert", None),
    )
    out_specs = (
        P("expert", "dp"),
        P("expert", "dp"),
        P("expert", None),
        P("expert", None, "dp"),
        P("expert", None, "dp"),
        P("expert", None, "dp"),
    )
    return jax.shard_map(body, mesh=mesh, in_specs=in_specs, out_specs=out_specs, check_vma=False)
```

profile of v0, /device:TPU:18, one launch (start us, length us, event | category | flops | bytes accessed | tf_op | source)
XLA Modules:
  0.0 721.3 jit_solution(9536386574595860201)
XLA Ops:
  12.3 24.4 %scatter_custom_fusion.1 = bf16[1536,2048]{1,0:T(8,128)(2,1)} fusion(s32[1024]{0:T(1024)S(1)} %get-tuple-element.14, f32[1024]{0:T(1024)S(1)} %mul.40, bf16[]{:T(256)} %constant.53.clone.1, bf16[128,2048]{1,0:T(8,128)(2,1)} %param.13, s32[1024]{0:T(1024)S(1)} %get-tuple-element.13), kind=kCustom, calls=%fused_computation.8 | custom fusion | flops 6291456 | bytes 6823938
  36.7 12.7 %copy.69 = bf16[2,64,12,2048]{3,0,2,1:T(2,128)(2,1)} copy(bf16[2,64,12,2048]{3,1,2,0:T(8,128)(2,1)} %bitcast.61) | data formatting | bytes 12582912 | tf_op jit(solution)/shard_map/scatter | solution.py:60
  49.4 9.4 %all-to-all-start.2 = ((bf16[2,64,12,2048]{3,0,2,1:T(2,128)(2,1)}), bf16[2,64,12,2048]{3,0,2,1:T(2,128)(2,1)}, u32[]{:S(2)}, u32[]{:S(2)}) async-start(bf16[2,64,12,2048]{3,0,2,1:T(2,128)(2,1)} %copy.69), calls=%async_computation.3 | async-start | bytes 12582912 | tf_op jit(solution)/shard_map/all_to_all | solution.py:79
  58.8 24.0 %scatter_custom_fusion = bf16[1536,2048]{1,0:T(8,128)(2,1)} fusion(s32[1024]{0:T(1024)S(1)} %get-tuple-element.14, bf16[128,2048]{1,0:T(8,128)(2,1)} %param.7, s32[1024]{0:T(1024)S(1)} %get-tuple-element.13, bf16[]{:T(256)} %constant.53.clone.1), kind=kCustom, calls=%fused_computation.9 | custom fusion | bytes 6291968
  82.8 12.7 %copy.63 = bf16[2,64,12,2048]{3,0,2,1:T(2,128)(2,1)} copy(bf16[2,64,12,2048]{3,1,2,0:T(8,128)(2,1)} %bitcast.60) | data formatting | bytes 12582912 | tf_op jit(solution)/shard_map/scatter | solution.py:60
  95.5 45.7 %all-to-all-done.2 = bf16[2,64,12,2048]{3,0,2,1:T(2,128)(2,1)} async-done(((bf16[2,64,12,2048]{3,0,2,1:T(2,128)(2,1)}), bf16[2,64,12,2048]{3,0,2,1:T(2,128)(2,1)}, u32[]{:S(2)}, u32[]{:S(2)}) %all-to-all-start.2) | async-done | bytes 6291488 | tf_op jit(solution)/shard_map/all_to_all | solution.py:79
  141.2 6.5 all-to-all-start
  147.7 16.1 %copy.75 = bf16[2,768,2048]{1,2,0:T(8,128)(2,1)} copy(bf16[2,768,2048]{2,0,1:T(2,128)(2,1)} %bitcast.15) | data formatting | bytes 12582912 | tf_op jit(solution)/shard_map/reshape | solution.py:82
  163.9 66.3 %all-to-all-done = bf16[2,64,12,2048]{3,0,2,1:T(2,128)(2,1)} async-done(((bf16[2,64,12,2048]{3,0,2,1:T(2,128)(2,1)}), bf16[2,64,12,2048]{3,0,2,1:T(2,128)(2,1)}, u32[]{:S(2)}, u32[]{:S(2)}) %all-to-all-start) | async-done | bytes 6291488 | tf_op jit(solution)/shard_map/all_to_all | solution.py:66
  230.1 16.2 %copy.73 = bf16[2,768,2048]{1,2,0:T(8,128)(2,1)} copy(bf16[2,768,2048]{2,0,1:T(2,128)(2,1)} %bitcast.7) | data formatting | bytes 12582912 | tf_op jit(solution)/shard_map/reshape | solution.py:69
  246.3 6.7 fusion.19
  257.9 7.3 %multiply_convert_fusion.2 = (bf16[2,768,384]{2,1,0:T(8,128)(2,1)}, bf16[2,768,384]{2,1,0:T(8,128)(2,1)}, bf16[2,768,384]{2,1,0:T(8,128)(2,1)}) fusion(f32[2,768,384]{2,1,0:T(8,128)} %fusion.18, f32[2,768,384]{2,1,0:T(8,128)S(1)} %fusion.19, bf16[2,768,2048]{1,2,0:T(8,128)(2,1)S(1)} %bitcast.65, bf16[2,2048,384]{2,1,0:T(8,128)(2,1)S(1)} %copy-done), kind=kOutput, calls=%fused_computation.17 | convolution fusion | flops 2424766464 | bytes 17694720 | tf_op jit(solution)/shard_map/jrd,jdf->jrf/dot_general | solution.py:19
  269.9 10.3 %convolution_add_fusion = f32[2,768,2048]{2,1,0:T(8,128)} fusion(f32[2,768,2048]{2,1,0:T(8,128)S(1)} %fusion.21, bf16[2,768,384]{2,1,0:T(8,128)(2,1)} %get-tuple-element.9, bf16[2,2048,384]{2,1,0:T(8,128)(2,1)} %param.11), kind=kOutput, calls=%fused_computation.7 | convolution fusion | flops 2419064832 | bytes 29491200 | tf_op jit(solution)/shard_map/jrf,jdf->jrd/dot_general | solution.py:25
  280.3 7.7 %fusion.20 = f32[2,768,2048]{2,1,0:T(8,128)} fusion(bf16[2,768,384]{2,1,0:T(8,128)(2,1)} %get-tuple-element.11, bf16[2,2048,384]{2,1,0:T(8,128)(2,1)S(1)} %copy-done), kind=kOutput, calls=%fused_computation.62 | convolution fusion | flops 2415919104 | bytes 16908288 | tf_op jit(solution)/shard_map/jrf,jdf->jrd/dot_general | solution.py:13
  288.0 141.3 %reduce-scatter.5.cloned.1.call-done = f32[2,768,1024]{2,1,0:T(8,128)} async-done(((f32[2,768,2048]{2,1,0:T(8,128)}), f32[2,768,1024]{2,1,0:T(8,128)}) %reduce-scatter.5.cloned.1.call-update) | async-done | bytes 6291472 | tf_op jit(solution)/shard_map/reduce_scatter | solution.py:86
  437.5 8.2 %all-to-all-start.3 = ((bf16[2,64,12,1024]{3,0,2,1:T(2,128)(2,1)}), bf16[2,64,12,1024]{3,0,2,1:T(2,128)(2,1)S(1)}, u32[]{:S(2)}, u32[]{:S(2)}) async-start(bf16[2,64,12,1024]{3,0,2,1:T(2,128)(2,1)} %bitcast.63), calls=%async_computation.5 | async-start | bytes 6291456 | tf_op jit(solution)/shard_map/all_to_all | solution.py:87
  445.7 167.6 %reduce-scatter.3.cloned.1.call-done = f32[2,768,1024]{2,1,0:T(8,128)} async-done(((f32[2,768,2048]{2,1,0:T(8,128)}), f32[2,768,1024]{2,1,0:T(8,128)}) %reduce-scatter.3.cloned.1.call-update) | async-done | bytes 6291472 | tf_op jit(solution)/shard_map/reduce_scatter | solution.py:71
  623.2 8.1 %all-to-all-start.1 = ((bf16[2,64,12,1024]{3,0,2,1:T(2,128)(2,1)}), bf16[2,64,12,1024]{3,0,2,1:T(2,128)(2,1)}, u32[]{:S(2)}, u32[]{:S(2)}) async-start(bf16[2,64,12,1024]{3,0,2,1:T(2,128)(2,1)} %bitcast.62), calls=%async_computation.2 | async-start | bytes 6291456 | tf_op jit(solution)/shard_map/all_to_all | solution.py:72
  632.4 8.3 %convolution_convert_fusion = bf16[2,2048,384]{2,1,0:T(8,128)(2,1)} fusion(bf16[2,768,2048]{1,2,0:T(8,128)(2,1)} %copy.75, bf16[2,768,384]{2,1,0:T(8,128)(2,1)} %get-tuple-element.11), kind=kOutput, calls=%fused_computation.12 | convolution fusion | flops 2417491968 | bytes 10616832 | tf_op jit(solution)/shard_map/jrd,jrf->jdf/dot_general | solution.py:28
  640.8 8.0 %convolution_convert_fusion.1 = bf16[2,2048,384]{2,1,0:T(8,128)(2,1)} fusion(bf16[2,768,2048]{1,2,0:T(8,128)(2,1)} %copy.73, bf16[2,768,384]{2,1,0:T(8,128)(2,1)S(1)} %copy-done.9), kind=kOutput, calls=%fused_computation.13 | convolution fusion | flops 2417491968 | bytes 10616832 | tf_op jit(solution)/shard_map/jrd,jrf->jdf/dot_general | solution.py:27
  655.4 16.6 %gather_fusion.1 = bf16[1024,1024]{1,0:T(8,128)(2,1)} fusion(bf16[2,64,12,1024]{3,1,2,0:T(8,128)(2,1)S(1)} %copy.72, s32[1024]{0:T(1024)S(1)} %bitcast.58), kind=kCustom, calls=%fused_computation.3 | custom fusion | bytes 4206592 | tf_op jit(solution)/shard_map/gather | solution.py:63
  675.8 5.3 copy.67
  681.1 21.4 %gather_fusion = bf16[1024,1024]{1,0:T(8,128)(2,1)} fusion(bf16[2,64,12,1024]{3,1,2,0:T(8,128)(2,1)} %copy.67, s32[1024]{0:T(1024)S(1)} %bitcast.59), kind=kCustom, calls=%fused_computation.1 | custom fusion | bytes 4206592 | tf_op jit(solution)/shard_map/gather | solution.py:63
  707.0 7.0 psum.7
  (76 shorter events, 48.8 us)
Async XLA Ops:
  7.2 250.7 %copy-start = (bf16[2,2048,384]{2,1,0:T(8,128)(2,1)S(1)}, bf16[2,2048,384]{2,1,0:T(8,128)(2,1)}, u32[]{:S(2)}) copy-start(bf16[2,2048,384]{2,1,0:T(8,128)(2,1)} %param.12) | copy-start | bytes 9437188
  7.2 4.9 copy-start.11
  7.2 5.0 copy-start.12
  9.6 0.8 copy-start.7
  49.4 91.8 %all-to-all-start.2 = ((bf16[2,64,12,2048]{3,0,2,1:T(2,128)(2,1)}), bf16[2,64,12,2048]{3,0,2,1:T(2,128)(2,1)}, u32[]{:S(2)}, u32[]{:S(2)}) async-start(bf16[2,64,12,2048]{3,0,2,1:T(2,128)(2,1)} %copy.69), calls=%async_computation.3 | async-start | bytes 12582912 | tf_op jit(solution)/shard_map/all_to_all | solution.py:79
  141.2 88.9 %all-to-all-start = ((bf16[2,64,12,2048]{3,0,2,1:T(2,128)(2,1)}), bf16[2,64,12,2048]{3,0,2,1:T(2,128)(2,1)}, u32[]{:S(2)}, u32[]{:S(2)}) async-start(bf16[2,64,12,2048]{3,0,2,1:T(2,128)(2,1)} %copy.63), calls=%async_computation | async-start | bytes 12582912 | tf_op jit(solution)/shard_map/all_to_all | solution.py:66
  147.7 281.6 %reduce-scatter.5.cloned.1.call-start = ((), (), s32[]{:S(2)}) async-start(), calls=%async_computation.7 | async-start | bytes 18874368 | tf_op jit(solution)/shard_map/reduce_scatter | solution.py:86
  246.3 6.7 copy-start.5
  246.3 6.7 copy-start.6
  246.3 11.6 %slice-start = ((s8[6291456]{0:T(1024)(128)(4,1)}), s8[4194304]{0:T(1024)(128)(4,1)S(1)}, s32[]{:S(2)}) async-start(s8[6291456]{0:T(1024)(128)(4,1)} %bitcast.64), calls=%async_computation.8 | async-start | bytes 8388608
  253.0 4.9 slice-start.1
  280.3 333.0 %reduce-scatter.3.cloned.1.call-start = ((), (), s32[]{:S(2)}) async-start(), calls=%async_computation.6 | async-start | bytes 18874368 | tf_op jit(solution)/shard_map/reduce_scatter | solution.py:71
  437.5 184.0 %all-to-all-start.3 = ((bf16[2,64,12,1024]{3,0,2,1:T(2,128)(2,1)}), bf16[2,64,12,1024]{3,0,2,1:T(2,128)(2,1)S(1)}, u32[]{:S(2)}, u32[]{:S(2)}) async-start(bf16[2,64,12,1024]{3,0,2,1:T(2,128)(2,1)} %bitcast.63), calls=%async_computation.5 | async-start | bytes 6291456 | tf_op jit(solution)/shard_map/all_to_all | solution.py:87
  621.5 1.7 copy-start.2
  621.5 9.8 %copy-start.10 = (f32[128,8]{0,1:T(8,128)S(1)}, f32[128,8]{0,1:T(8,128)}, u32[]{:S(2)}) copy-start(f32[128,8]{0,1:T(8,128)} %param.9) | copy-start | bytes 12292
  623.2 52.6 %all-to-all-start.1 = ((bf16[2,64,12,1024]{3,0,2,1:T(2,128)(2,1)}), bf16[2,64,12,1024]{3,0,2,1:T(2,128)(2,1)}, u32[]{:S(2)}, u32[]{:S(2)}) async-start(bf16[2,64,12,1024]{3,0,2,1:T(2,128)(2,1)} %bitcast.62), calls=%async_computation.2 | async-start | bytes 6291456 | tf_op jit(solution)/shard_map/all_to_all | solution.py:72
  632.4 8.4 %copy-start.9 = (bf16[2,768,384]{2,1,0:T(8,128)(2,1)S(1)}, bf16[2,768,384]{2,1,0:T(8,128)(2,1)}, u32[]{:S(2)}) copy-start(bf16[2,768,384]{2,1,0:T(8,128)(2,1)} %get-tuple-element.9) | copy-start | bytes 3538948
  632.4 16.4 %slice-start.2 = ((s8[6291456]{0:T(1024)(128)(4,1)}), s8[4194304]{0:T(1024)(128)(4,1)S(1)}, s32[]{:S(2)}) async-start(s8[6291456]{0:T(1024)(128)(4,1)} %bitcast.66), calls=%async_computation.10 | async-start | bytes 8388608
  640.8 8.0 %slice-start.3 = ((s8[6291456]{0:T(1024)(128)(4,1)}), s8[2097152]{0:T(1024)(128)(4,1)S(1)}, s32[]{:S(2)}) async-start(s8[6291456]{0:T(1024)(128)(4,1)} %bitcast.66), calls=%async_computation.11 | async-start | bytes 4194304
  640.8 8.0 %copy-start.8 = (bf16[2,768,384]{2,1,0:T(8,128)(2,1)S(1)}, bf16[2,768,384]{2,1,0:T(8,128)(2,1)}, u32[]{:S(2)}) copy-start(bf16[2,768,384]{2,1,0:T(8,128)(2,1)} %get-tuple-element.10) | copy-start | bytes 3538948
  648.8 4.8 copy-start.3
  681.1 33.0 %copy-start.1 = (bf16[2,2048,384]{2,1,0:T(8,128)(2,1)S(1)}, bf16[2,2048,384]{2,1,0:T(8,128)(2,1)}, u32[]{:S(2)}) copy-start(bf16[2,2048,384]{2,1,0:T(8,128)(2,1)} %param.12) | copy-start | bytes 9437188
  702.5 3.0 copy-start.4
Sparse Core Ops, SparseCore 0:
  280.4 148.8 reduce-scatter.4
  431.7 181.5 reduce-scatter.2
where the time goes:
time: 732 us; the launch traced here: 721 us
  waiting for transfers between devices  421 us (58%)
  local copies, waits for them, and re-layouts  143 us (20%)
  matrix products  66.4 us (9%)
  other arithmetic  36.6 us (5%)
  starting transfers between devices  32.2 us (4%)
  between operations  14.8 us (2%)
    reduce_scatter x1, waiting for transfers between devices, body(): out_sum = lax.psum_scatter(out_part, 'dp', scatter_dimension=2, tiled=True)  168 us
    reduce_scatter x1, waiting for transfers between devices, body(): row_sum = lax.psum_scatter(row_part, 'dp', scatter_dimension=2, tiled=True)  141 us
    all_to_all x1, waiting for transfers between devices, body(): lax.all_to_all(scatter_rows(x_rows), 'expert', split_axis=1, concat_axis=...  66.3 us
    all_to_all x1, waiting for transfers between devices, body(): lax.all_to_all(scatter_rows(weighted), 'expert', split_axis=1, concat_axi...  45.7 us
    gather x2, local copies, waits for them, and re-layouts, gather_rows(): return buffer[slots, owners, within]  38.1 us
    unnamed x38, local copies, waits for them, and re-layouts  28.4 us
    scatter x2, local copies, waits for them, and re-layouts, scatter_rows(): return buffer.at[slots, owners, within].set(values)  25.4 us
    unnamed x5, other arithmetic  24.6 us
  transfers between devices with their start and end apart: 6, of which 4 were waited for; matrix products, arithmetic and copies ran while one was open for 17% of the time, Pallas kernels for 0%

commit v1 on v0

v1 whole, which is shorter than its diff:
```python
import functools

import jax
import jax.numpy as jnp
from jax import lax
from jax.experimental import pallas as pl
from jax.experimental.pallas import tpu as pltpu
from jax.sharding import PartitionSpec as P

BF = jnp.bfloat16
F32 = jnp.float32
TN = (((0,), (0,)), ((), ()))
NT = (((1,), (1,)), ((), ()))
LIMIT = 48 * 2**20


def dot(a, b, dims=(((1,), (0,)), ((), ())), precision=None):
    return lax.dot_general(a, b, dims, precision=precision, preferred_element_type=F32)


def iota(shape, dim):
    return lax.broadcasted_iota(jnp.int32, shape, dim)


def slot_experts(first, rows, experts, capacity):
    slot = first + iota((rows, experts), 0)
    low = iota((rows, experts), 1) * capacity
    return (slot >= low) & (slot < low + capacity)


def pack_rows_kernel(capacity, picks_ref, tokens_ref, rows_ref, place_ref, rank_ref):
    step = pl.program_id(0)
    experts, toks = rank_ref.shape
    rows = rows_ref.shape[0]

    @pl.when(step == 0)
    def _():
        named = jnp.zeros((experts, toks), F32)
        for k in range(picks_ref.shape[0]):
            named += (iota((experts, toks), 0) == picks_ref[k : k + 1, :]).astype(F32)
        before = (iota((toks, toks), 0) < iota((toks, toks), 1)).astype(F32).astype(BF)
        rank = dot(named.astype(BF), before)
        rank_ref[...] = jnp.where(named > 0, rank, -1.0).astype(BF)

    first = step * rows
    chosen = slot_experts(first, rows, experts, capacity).astype(F32).astype(BF)
    slot = (first + iota((rows, toks), 0)).astype(F32)
    within = slot - capacity * jnp.floor((slot + 0.5) * (1.0 / capacity))
    place = (dot(chosen, rank_ref[...]) == within).astype(F32).astype(BF)
    place_ref[...] = place
    rows_ref[...] = dot(place, tokens_ref[...]).astype(BF)


def pack_rows(picks, tokens, capacity, experts, steps=4):
    toks, width = tokens.shape
    slots = experts * capacity
    rows = slots // steps
    return pl.pallas_call(
        functools.partial(pack_rows_kernel, capacity),
        grid=(steps,),
        in_specs=[
            pl.BlockSpec(picks.shape, lambda i: (0, 0)),
            pl.BlockSpec((toks, width), lambda i: (0, 0)),
        ],
        out_specs=[
            pl.BlockSpec((rows, width), lambda i: (i, 0)),
            pl.BlockSpec((rows, toks), lambda i: (i, 0)),
        ],
        out_shape=[
            jax.ShapeDtypeStruct((slots, width), BF),
            jax.ShapeDtypeStruct((slots, toks), BF),
        ],
        scratch_shapes=[pltpu.VMEM((experts, toks), BF)],
        compiler_params=pltpu.CompilerParams(vmem_limit_bytes=LIMIT),
        cost_estimate=pl.CostEstimate(
            flops=2 * slots * toks * width, bytes_accessed=2 * slots * width, transcendentals=0
        ),
        name="pack_rows",
    )(picks, tokens)


def pack_back_kernel(capacity, picks_ref, gates_ref, place_ref, cot_ref, rows_ref, high_ref, low_ref, by_ref):
    step = pl.program_id(0)
    experts, toks = by_ref.shape
    rows = rows_ref.shape[0]

    @pl.when(step == 0)
    def _():
        by = jnp.zeros((experts, toks), F32)
        for k in range(picks_ref.shape[0]):
            by += jnp.where(iota((experts, toks), 0) == picks_ref[k : k + 1, :], gates_ref[k : k + 1, :], 0.0)
        by_ref[...] = by

    chosen = slot_experts(step * rows, rows, experts, capacity).astype(F32)
    place = place_ref[...]
    weight = place.astype(F32) * dot(chosen, by_ref[...], precision=lax.Precision.HIGHEST)
    high = weight.astype(BF)
    high_ref[...] = high
    low_ref[...] = (weight - high.astype(F32)).astype(BF)
    scale = jnp.sum(weight, axis=1, keepdims=True)
    rows_ref[...] = (scale * dot(place, cot_ref[...])).astype(BF)


def pack_back(picks, gates, place, cot, capacity, experts, steps=4):
    toks, width = cot.shape
    slots = experts * capacity
    rows = slots // steps
    whole = lambda i: (0, 0)
    part = lambda i: (i, 0)
    return pl.pallas_call(
        functools.partial(pack_back_kernel, capacity),
        grid=(steps,),
        in_specs=[
            pl.BlockSpec(picks.shape, whole),
            pl.BlockSpec(gates.shape, whole),
            pl.BlockSpec((rows, toks), part),
            pl.BlockSpec((toks, width), whole),
        ],
        out_specs=[
            pl.BlockSpec((rows, width), part),
            pl.BlockSpec((rows, toks), part),
            pl.BlockSpec((rows, toks), part),
        ],
        out_shape=[
            jax.ShapeDtypeStruct((slots, width), BF),
            jax.ShapeDtypeStruct((slots, toks), BF),
            jax.ShapeDtypeStruct((slots, toks), BF),
        ],
        scratch_shapes=[pltpu.VMEM((experts, toks), F32)],
        compiler_params=pltpu.CompilerParams(vmem_limit_bytes=LIMIT),
        cost_estimate=pl.CostEstimate(
            flops=2 * slots * toks * width, bytes_accessed=2 * slots * width, transcendentals=0
        ),
        name="pack_back",
    )(picks, gates, place, cot)


def mix_kernel(capacity, experts, picks_ref, place_ref, high_ref, low_ref, cot_ref, rows_ref, mixed_ref, gates_ref, along_ref):
    step = pl.program_id(0)
    rows = rows_ref[...]
    mixed_ref[...] = dot(high_ref[...], rows, TN) + dot(low_ref[...], rows, TN)
    along = dot(rows, cot_ref[...], NT)

    @pl.when(step == 0)
    def _():
        along_ref[...] = along

    @pl.when(step > 0)
    def _():
        along_ref[...] += along

    @pl.when(step == pl.num_programs(0) - 1)
    def _():
        slots, toks = along_ref.shape
        chosen = slot_experts(0, slots, experts, capacity).astype(F32)
        kept = along_ref[...] * place_ref[...].astype(F32)
        by = dot(chosen, kept, TN, precision=lax.Precision.HIGHEST)
        for k in range(picks_ref.shape[0]):
            mine = jnp.where(iota((experts, toks), 0) == picks_ref[k : k + 1, :], by, 0.0)
            gates_ref[k : k + 1, :] = jnp.sum(mine, axis=0, keepdims=True)


def mix(picks, place, high, low, cot, rows, capacity, experts, steps=4):
    toks, width = cot.shape
    slots = experts * capacity
    cols = width // steps
    whole = lambda i: (0, 0)
    part = lambda i: (0, i)
    return pl.pallas_call(
        functools.partial(mix_kernel, capacity, experts),
        grid=(steps,),
        in_specs=[
            pl.BlockSpec(picks.shape, whole),
            pl.BlockSpec((slots, toks), whole),
            pl.BlockSpec((slots, toks), whole),
            pl.BlockSpec((slots, toks), whole),
            pl.BlockSpec((toks, cols), part),
            pl.BlockSpec((slots, cols), part),
        ],
        out_specs=[pl.BlockSpec((toks, cols), part), pl.BlockSpec(picks.shape, whole)],
        out_shape=[
            jax.ShapeDtypeStruct((toks, width), F32),
            jax.ShapeDtypeStruct(picks.shape, F32),
        ],
        scratch_shapes=[pltpu.VMEM((slots, toks), F32)],
        compiler_params=pltpu.CompilerParams(vmem_limit_bytes=LIMIT),
        cost_estimate=pl.CostEstimate(
            flops=6 * slots * toks * width, bytes_accessed=2 * slots * width, transcendentals=0
        ),
        name="mix",
    )(picks, place, high, low, cot, rows)


def sum_rows_kernel(place_ref, rows_ref, out_ref):
    out_ref[...] = dot(place_ref[...], rows_ref[...], TN)


def sum_rows(place, rows, steps=4):
    slots, toks = place.shape
    width = rows.shape[1]
    cols = width // steps
    return pl.pallas_call(
        sum_rows_kernel,
        grid=(steps,),
        in_specs=[
            pl.BlockSpec((slots, toks), lambda i: (0, 0)),
            pl.BlockSpec((slots, cols), lambda i: (0, i)),
        ],
        out_specs=pl.BlockSpec((toks, cols), lambda i: (0, i)),
        out_shape=jax.ShapeDtypeStruct((toks, width), F32),
        compiler_params=pltpu.CompilerParams(vmem_limit_bytes=LIMIT),
        cost_estimate=pl.CostEstimate(
            flops=2 * slots * toks * width, bytes_accessed=2 * slots * width, transcendentals=0
        ),
        name="sum_rows",
    )(place, rows)


def exchange(rows):
    return lax.all_to_all(rows, "expert", split_axis=0, concat_axis=0, tiled=True)


def other(value):
    return lax.ppermute(value, "dp", [(0, 1), (1, 0)])


def add_over_dp(part):
    half = part.shape[1] // 2
    member = lax.axis_index("dp")
    away = lax.dynamic_slice_in_dim(part, (1 - member) * half, half, 1).astype(BF)
    kept = lax.dynamic_slice_in_dim(part, member * half, half, 1)
    return (kept + other(away).astype(F32)).astype(BF)


def body(tokens, routing, route_gates, gate_weight, up_weight, down_weight, cotangent):
    toks, width = tokens.shape
    local = gate_weight.shape[0]
    experts = local * lax.axis_size("expert")
    capacity = 3 * toks * routing.shape[1] // (2 * experts)
    slots = experts * capacity
    picks, gates = routing.T, route_gates.T

    sent_rows, place = pack_rows(picks, tokens, capacity, experts)
    x = exchange(sent_rows)
    sent_back, high, low = pack_back(picks, gates, place, cotangent, capacity, experts)
    back = exchange(sent_back)

    second = (iota((slots, 1), 0) // capacity) % local == 1

    def by_expert(rows, weight, dims=(((1,), (0,)), ((), ()))):
        return jnp.where(second, dot(rows, weight[1], dims), dot(rows, weight[0], dims))

    def halves(value):
        zero = jnp.zeros((), value.dtype)
        return jnp.where(second, zero, value), jnp.where(second, value, zero)

    gate_pre = by_expert(x, gate_weight)
    up_pre = by_expert(x, up_weight)
    s = jax.nn.sigmoid(gate_pre)
    active = gate_pre * s
    hidden = halves((active * up_pre).astype(BF))
    out = (dot(hidden[0], down_weight[0], NT) + dot(hidden[1], down_weight[1], NT)).astype(BF)
    back, out = lax.optimization_barrier((back, out))
    got_out = exchange(out)

    dhidden = by_expert(back, down_weight)
    d_gate = halves((dhidden * up_pre * s * (1.0 + gate_pre * (1.0 - s))).astype(BF))
    d_up = halves((dhidden * active).astype(BF))
    row = sum(
        dot(d_gate[j], gate_weight[j], NT) + dot(d_up[j], up_weight[j], NT) for j in range(local)
    ).astype(BF)
    row, got_out = lax.optimization_barrier((row, got_out))
    got_row = exchange(row)

    mixed_part, gates_part = mix(picks, place, high, low, cotangent, got_out, capacity, experts)
    mixed = add_over_dp(mixed_part)
    gates_grad = (gates_part + other(gates_part)).T
    token_grad = add_over_dp(sum_rows(place, got_row))

    def outer(rows, values):
        return jnp.stack([dot(rows, values[j], TN).astype(BF) for j in range(local)])

    return (
        mixed,
        token_grad,
        gates_grad,
        outer(x, d_gate),
        outer(x, d_up),
        outer(back, hidden),
    )


def solution(mesh):
    by_dp = P("expert", None, "dp")
    rows = P("expert", None)
    in_specs = (rows, rows, rows, by_dp, by_dp, by_dp, rows)
    out_specs = (P("expert", "dp"), P("expert", "dp"), rows, by_dp, by_dp, by_dp)
    return jax.shard_map(body, mesh=mesh, in_specs=in_specs, out_specs=out_specs, check_vma=False)
```

time: 732 us -> 386 us (0.53)
  waiting for transfers between devices: 421 us -> 186 us
  local copies, waits for them, and re-layouts: 143 us -> 1.88 us
  matrix products: 66.4 us -> 127 us
  other arithmetic: 36.6 us -> 7.26 us
  Pallas kernels: 0 us -> 20.8 us
  between operations: 14.8 us -> 1.18 us
    reduce_scatter x2 -> x0, waiting for transfers between devices: 309 us -> none  [the longest x1 168 us: body(): out_sum = lax.psum_scatter(out_part, 'dp', scatter_dimension=2, tiled=True)]
    all_to_all x4, waiting for transfers between devices: 112 us -> 181 us  [exchange(): lax.all_to_all(rows, 'expert', split_axis=0, concat_axis=0, tiled=True)]
    dot_general x11 -> x18, matrix products: 66.4 us -> 127 us  [dot(): lax.dot_general(a, b, dims, precision=precision, preferred_element_type=F32)]
    gather x2 -> x0, local copies, waits for them, and re-layouts: 38.1 us -> none  [gather_rows(): return buffer[slots, owners, within]]
    reshape x3 -> x0, local copies, waits for them, and re-layouts: 32.4 us -> none  [the longest x1 16.2 us: body(): slot_rows = got_rows.reshape(local_count, devices * capacity, width)]
    unnamed x38 -> x36, local copies, waits for them, and re-layouts: 28.4 us -> 1.81 us
    scatter x2 -> x0, local copies, waits for them, and re-layouts: 25.4 us -> none  [scatter_rows(): return buffer.at[slots, owners, within].set(values)]
    unnamed x5 -> x0, other arithmetic: 24.6 us -> none
  transfers between devices with their start and end apart: 6 -> 7, of which waited for: 4 -> 5; matrix products, arithmetic and copies ran while one was open for 17% -> 35% of each run, Pallas kernels for 0% -> 4%
where the time goes in v1:
time: 386 us; the launch traced here: 382 us
  waiting for transfers between devices  186 us (48%)
  matrix products  127 us (33%)
  starting transfers between devices  39 us (10%)
  Pallas kernels  20.8 us (5%)
  other arithmetic  7.26 us (2%)
    all_to_all x4, waiting for transfers between devices, exchange(): lax.all_to_all(rows, 'expert', split_axis=0, concat_axis=0, tiled=True)  181 us
    dot_general x18, matrix products, dot(): lax.dot_general(a, b, dims, precision=precision, preferred_element_type=F32)  127 us
    all_to_all x4, starting transfers between devices, exchange(): lax.all_to_all(rows, 'expert', split_axis=0, concat_axis=0, tiled=True)  31.6 us
  transfers between devices with their start and end apart: 7, of which 5 were waited for; matrix products, arithmetic and copies ran while one was open for 35% of the time, Pallas kernels for 4%

profile of v1, /device:TPU:18, one launch (start us, length us, event | category | flops | bytes accessed | tf_op | source)
XLA Modules:
  0.0 382.4 jit_solution(18401735471482150909)
XLA Ops:
  6.9 9.5 %all-to-all-start.1 = ((bf16[64,24,2048]{2,1,0:T(8,128)(2,1)}), bf16[64,24,2048]{2,1,0:T(8,128)(2,1)}, u32[]{:S(2)}, u32[]{:S(2)}) async-start(bf16[64,24,2048]{2,1,0:T(8,128)(2,1)} %bitcast.77), calls=%async_computation.1 | async-start | bytes 12582912 | tf_op jit(solution)/shard_map/all_to_all | solution.py:220
  21.1 77.7 %all-to-all-done.1 = bf16[64,24,2048]{2,1,0:T(8,128)(2,1)} async-done(((bf16[64,24,2048]{2,1,0:T(8,128)(2,1)}), bf16[64,24,2048]{2,1,0:T(8,128)(2,1)}, u32[]{:S(2)}, u32[]{:S(2)}) %all-to-all-start.1) | async-done | bytes 6291488 | tf_op jit(solution)/shard_map/all_to_all | solution.py:220
  98.9 7.1 %all-to-all-start = ((bf16[64,24,2048]{2,1,0:T(8,128)(2,1)}), bf16[64,24,2048]{2,1,0:T(8,128)(2,1)}, u32[]{:S(2)}, u32[]{:S(2)}) async-start(bf16[64,24,2048]{2,1,0:T(8,128)(2,1)} %bitcast.76), calls=%async_computation | async-start | bytes 12582912 | tf_op jit(solution)/shard_map/all_to_all | solution.py:220
  106.0 6.1 %fusion.24 = f32[1536,384]{1,0:T(8,128)S(1)} fusion(bf16[1536,2048]{1,0:T(8,128)(2,1)} %bitcast.5, bf16[2,2048,384]{2,1,0:T(8,128)(2,1)} %param.10), kind=kOutput, calls=%fused_computation.42 | convolution fusion | flops 2415919104 | bytes 10223616 | tf_op jit(solution)/shard_map/dot_general | solution.py:18
  123.5 8.8 %multiply_convert_fusion.2 = (bf16[1536,384]{1,0:T(8,128)(2,1)S(1)}, f32[1536,384]{1,0:T(8,128)}) fusion(f32[1536,384]{1,0:T(8,128)S(1)} %convolution_select_fusion.2, f32[1536,384]{1,0:T(8,128)S(1)} %fusion.17, bf16[1536,2048]{1,0:T(8,128)(2,1)} %bitcast.5, bf16[2,2048,384]{2,1,0:T(8,128)(2,1)S(1)} %copy-done.9, pred[1536]{0:T(1024)(128)(4,1)S(1)} %fusion.39), kind=kOutput, calls=%fused_computation.22 | convolution fusion | flops 2420047872 | bytes 16123904 | tf_op jit(solution)/shard_map/dot_general | solution.py:18
  135.9 7.2 %add_convert_fusion.1 = bf16[1536,2048]{1,0:T(8,128)(2,1)} fusion(f32[1536,2048]{1,0:T(8,128)S(1)} %fusion.11, bf16[2,2048,384]{2,1,0:T(8,128)(2,1)} %param.12, bf16[1536,384]{1,0:T(8,128)(2,1)S(1)} %get-tuple-element.30, pred[1536]{0:T(1024)(128)(4,1)S(1)} %fusion.39), kind=kOutput, calls=%fused_computation.1 | convolution fusion | flops 2422800384 | bytes 21628416 | tf_op jit(solution)/shard_map/dot_general | solution.py:18
  143.0 45.0 %all-to-all-done = bf16[64,24,2048]{2,1,0:T(8,128)(2,1)} async-done(((bf16[64,24,2048]{2,1,0:T(8,128)(2,1)}), bf16[64,24,2048]{2,1,0:T(8,128)(2,1)}, u32[]{:S(2)}, u32[]{:S(2)}) %all-to-all-start) | async-done | bytes 6291488 | tf_op jit(solution)/shard_map/all_to_all | solution.py:220
  188.0 7.5 %all-to-all-start.2 = ((bf16[64,24,2048]{2,1,0:T(8,128)(2,1)}), bf16[64,24,2048]{2,1,0:T(8,128)(2,1)}, u32[]{:S(2)}, u32[]{:S(2)}) async-start(bf16[64,24,2048]{2,1,0:T(8,128)(2,1)} %bitcast.74), calls=%async_computation.2 | async-start | bytes 12582912 | tf_op jit(solution)/shard_map/all_to_all | solution.py:220
  195.5 6.1 %fusion.7 = f32[1536,384]{1,0:T(8,128)S(1)} fusion(bf16[1536,2048]{1,0:T(8,128)(2,1)} %bitcast.3, bf16[2,2048,384]{2,1,0:T(8,128)(2,1)} %param.12), kind=kOutput, calls=%fused_computation.25 | convolution fusion | flops 2415919104 | bytes 10223616 | tf_op jit(solution)/shard_map/dot_general | solution.py:18
  201.7 7.4 %multiply_convert_fusion = (bf16[1536,384]{1,0:T(8,128)(2,1)S(1)}, bf16[1536,384]{1,0:T(8,128)(2,1)S(1)}) fusion(f32[1536,384]{1,0:T(8,128)S(1)} %copy-done.16, f32[1536,384]{1,0:T(8,128)S(1)} %copy-done.17, f32[1536,384]{1,0:T(8,128)S(1)} %fusion.7, bf16[1536,2048]{1,0:T(8,128)(2,1)} %bitcast.3, bf16[2,2048,384]{2,1,0:T(8,128)(2,1)S(1)} %copy-done.12, ...), kind=kOutput, calls=%fused_computation.20 | convolution fusion | flops 2424176640 | bytes 17303552 | tf_op jit(solution)/shard_map/dot_general | solution.py:18
  209.1 6.7 %fusion.19 = f32[1536,2048]{1,0:T(8,128)} fusion(bf16[2,2048,384]{2,1,0:T(8,128)(2,1)S(1)} %copy-done.14, bf16[1536,384]{1,0:T(8,128)(2,1)S(1)} %get-tuple-element.29, pred[1536]{0:T(1024)(128)(4,1)S(1)} %fusion.39), kind=kOutput, calls=%fused_computation.37 | convolution fusion | flops 2416508928 | bytes 15337472 | tf_op jit(solution)/shard_map/dot_general | solution.py:18
  215.8 6.7 %fusion.22 = f32[1536,2048]{1,0:T(8,128)} fusion(bf16[2,2048,384]{2,1,0:T(8,128)(2,1)S(1)} %copy-done.14, bf16[1536,384]{1,0:T(8,128)(2,1)S(1)} %get-tuple-element.29, pred[1536]{0:T(1024)(128)(4,1)S(1)} %fusion.39), kind=kOutput, calls=%fused_computation.40 | convolution fusion | flops 2416508928 | bytes 15337472 | tf_op jit(solution)/shard_map/dot_general | solution.py:18
  222.5 6.8 %fusion.13 = f32[1536,2048]{1,0:T(8,128)} fusion(bf16[2,2048,384]{2,1,0:T(8,128)(2,1)S(1)} %copy-done.10, bf16[1536,384]{1,0:T(8,128)(2,1)S(1)} %get-tuple-element.28, pred[1536]{0:T(1024)(128)(4,1)S(1)} %fusion.39), kind=kOutput, calls=%fused_computation.31 | convolution fusion | flops 2416508928 | bytes 15337472 | tf_op jit(solution)/shard_map/dot_general | solution.py:18
  229.2 17.4 %add_convert_fusion = bf16[1536,2048]{1,0:T(8,128)(2,1)} fusion(f32[1536,2048]{1,0:T(8,128)} %fusion.22, f32[1536,2048]{1,0:T(8,128)} %fusion.19, f32[1536,2048]{1,0:T(8,128)} %fusion.13, bf16[2,2048,384]{2,1,0:T(8,128)(2,1)} %param.11, bf16[1536,384]{1,0:T(8,128)(2,1)} %copy-done.7, pred[1536]{0:T(1024)(128)(4,1)S(1)} %fusion.39), kind=kOutput, calls=%fused_computation | convolution fusion | flops 2429091840 | bytes 46794240 | tf_op jit(solution)/shard_map/dot_general | solution.py:18
  246.6 30.8 %all-to-all-done.2 = bf16[64,24,2048]{2,1,0:T(8,128)(2,1)} async-done(((bf16[64,24,2048]{2,1,0:T(8,128)(2,1)}), bf16[64,24,2048]{2,1,0:T(8,128)(2,1)}, u32[]{:S(2)}, u32[]{:S(2)}) %all-to-all-start.2) | async-done | bytes 6291488 | tf_op jit(solution)/shard_map/all_to_all | solution.py:220
  277.5 7.5 %all-to-all-start.3 = ((bf16[64,24,2048]{2,1,0:T(8,128)(2,1)}), bf16[64,24,2048]{2,1,0:T(8,128)(2,1)}, u32[]{:S(2)}, u32[]{:S(2)}) async-start(bf16[64,24,2048]{2,1,0:T(8,128)(2,1)} %bitcast.75), calls=%async_computation.3 | async-start | bytes 12582912 | tf_op jit(solution)/shard_map/all_to_all | solution.py:220
  285.0 6.7 %fusion.4 = bf16[1,2048,384]{2,1,0:T(8,128)(2,1)S(1)} fusion(bf16[1536,2048]{1,0:T(8,128)(2,1)} %bitcast.3, bf16[1536,384]{1,0:T(8,128)(2,1)} %copy-done.5, pred[1536]{0:T(1024)(128)(4,1)S(1)} %fusion.39), kind=kOutput, calls=%fused_computation.18 | convolution fusion | flops 2417295360 | bytes 9045504 | tf_op jit(solution)/shard_map/dot_general | solution.py:18
  291.7 6.3 %fusion.5 = bf16[1,2048,384]{2,1,0:T(8,128)(2,1)S(1)} fusion(bf16[1536,2048]{1,0:T(8,128)(2,1)} %bitcast.3, bf16[1536,384]{1,0:T(8,128)(2,1)S(1)} %copy-done.6, pred[1536]{0:T(1024)(128)(4,1)S(1)} %fusion.39), kind=kOutput, calls=%fused_computation.19 | convolution fusion | flops 2417295360 | bytes 9045504 | tf_op jit(solution)/shard_map/dot_general | solution.py:18
  300.1 6.3 %fusion = bf16[1,2048,384]{2,1,0:T(8,128)(2,1)S(1)} fusion(bf16[1536,2048]{1,0:T(8,128)(2,1)} %bitcast.5, bf16[1536,384]{1,0:T(8,128)(2,1)S(1)} %get-tuple-element.29, pred[1536]{0:T(1024)(128)(4,1)S(1)} %fusion.39), kind=kOutput, calls=%fused_computation.14 | convolution fusion | flops 2417295360 | bytes 9045504 | tf_op jit(solution)/shard_map/dot_general | solution.py:18
  306.4 6.6 %fusion.1 = bf16[1,2048,384]{2,1,0:T(8,128)(2,1)S(1)} fusion(bf16[1536,2048]{1,0:T(8,128)(2,1)} %bitcast.5, bf16[1536,384]{1,0:T(8,128)(2,1)S(1)} %get-tuple-element.29, pred[1536]{0:T(1024)(128)(4,1)S(1)} %fusion.39), kind=kOutput, calls=%fused_computation.15 | convolution fusion | flops 2417295360 | bytes 9045504 | tf_op jit(solution)/shard_map/dot_general | solution.py:18
  313.1 6.3 %fusion.2 = bf16[1,2048,384]{2,1,0:T(8,128)(2,1)S(1)} fusion(bf16[1536,2048]{1,0:T(8,128)(2,1)} %bitcast.5, bf16[1536,384]{1,0:T(8,128)(2,1)S(1)} %copy-done.8, pred[1536]{0:T(1024)(128)(4,1)S(1)} %fusion.39), kind=kOutput, calls=%fused_computation.16 | convolution fusion | flops 2417295360 | bytes 9045504 | tf_op jit(solution)/shard_map/dot_general | solution.py:18
  319.4 6.3 %fusion.3 = bf16[1,2048,384]{2,1,0:T(8,128)(2,1)S(1)} fusion(bf16[1536,2048]{1,0:T(8,128)(2,1)} %bitcast.5, bf16[1536,384]{1,0:T(8,128)(2,1)S(1)} %copy-done.8, pred[1536]{0:T(1024)(128)(4,1)S(1)} %fusion.39), kind=kOutput, calls=%fused_computation.17 | convolution fusion | flops 2417295360 | bytes 9045504 | tf_op jit(solution)/shard_map/dot_general | solution.py:18
  328.8 7.3 %mix.1 = (f32[128,2048]{1,0:T(8,128)S(1)}, f32[8,128]{1,0:T(8,128)S(1)}) custom-call(s32[8,128]{1,0:T(8,128)S(1)} %bitcast.73, bf16[1536,128]{1,0:T(8,128)(2,1)S(1)} %get-tuple-element.17.place_ref, bf16[1536,128]{1,0:T(8,128)(2,1)S(1)} %get-tuple-element.18.high_ref, bf16[1536,128]{1,0:T(8,128)(2,1)S(1)} %get-tuple-element.19.low_ref, ...), custom_call_target="tpu_custom_call" | custom-call | flops 2415919104 | bytes 6291456 | tf_op jit(solution)/shard_map/mix/pallas_call | solution.py:169
  339.9 27.1 %all-to-all-done.3 = bf16[64,24,2048]{2,1,0:T(8,128)(2,1)} async-done(((bf16[64,24,2048]{2,1,0:T(8,128)(2,1)}), bf16[64,24,2048]{2,1,0:T(8,128)(2,1)}, u32[]{:S(2)}, u32[]{:S(2)}) %all-to-all-start.3) | async-done | bytes 6291488 | tf_op jit(solution)/shard_map/all_to_all | solution.py:220
  (56 shorter events, 49.9 us)
Async XLA Ops:
  0.6 1.0 copy-start
  6.9 9.5 %copy-start.1 = (bf16[128,2048]{1,0:T(8,128)(2,1)S(1)}, bf16[128,2048]{1,0:T(8,128)(2,1)}, u32[]{:S(2)}) copy-start(bf16[128,2048]{1,0:T(8,128)(2,1)} %cot_ref.3) | copy-start | bytes 1572868
  6.9 9.5 %copy-start.2 = (f32[128,8]{0,1:T(8,128)S(1)}, f32[128,8]{0,1:T(8,128)}, u32[]{:S(2)}) copy-start(f32[128,8]{0,1:T(8,128)} %param.9) | copy-start | bytes 12292
  6.9 9.5 %copy-start.4 = (s32[128,8]{0,1:T(8,128)S(1)}, s32[128,8]{0,1:T(8,128)}, u32[]{:S(2)}) copy-start(s32[128,8]{0,1:T(8,128)} %param.8) | copy-start | bytes 12292
  6.9 91.9 %all-to-all-start.1 = ((bf16[64,24,2048]{2,1,0:T(8,128)(2,1)}), bf16[64,24,2048]{2,1,0:T(8,128)(2,1)}, u32[]{:S(2)}, u32[]{:S(2)}) async-start(bf16[64,24,2048]{2,1,0:T(8,128)(2,1)} %bitcast.77), calls=%async_computation.1 | async-start | bytes 12582912 | tf_op jit(solution)/shard_map/all_to_all | solution.py:220
  98.9 89.1 %all-to-all-start = ((bf16[64,24,2048]{2,1,0:T(8,128)(2,1)}), bf16[64,24,2048]{2,1,0:T(8,128)(2,1)}, u32[]{:S(2)}, u32[]{:S(2)}) async-start(bf16[64,24,2048]{2,1,0:T(8,128)(2,1)} %bitcast.76), calls=%async_computation | async-start | bytes 12582912 | tf_op jit(solution)/shard_map/all_to_all | solution.py:220
  106.0 6.1 %copy-start.9 = (bf16[2,2048,384]{2,1,0:T(8,128)(2,1)S(1)}, bf16[2,2048,384]{2,1,0:T(8,128)(2,1)}, u32[]{:S(2)}) copy-start(bf16[2,2048,384]{2,1,0:T(8,128)(2,1)} %param.11) | copy-start | bytes 9437188
  112.1 5.7 %copy-start.13 = (bf16[2,2048,384]{2,1,0:T(8,128)(2,1)S(1)}, bf16[2,2048,384]{2,1,0:T(8,128)(2,1)}, u32[]{:S(2)}) copy-start(bf16[2,2048,384]{2,1,0:T(8,128)(2,1)} %param.10) | copy-start | bytes 9437188
  123.5 8.8 %copy-start.15 = (f32[1536,384]{1,0:T(8,128)}, f32[1536,384]{1,0:T(8,128)S(1)}, u32[]{:S(2)}) copy-start(f32[1536,384]{1,0:T(8,128)S(1)} %convolution_select_fusion.2) | copy-start | bytes 7077892
  123.5 8.8 %copy-start.11 = (bf16[2,2048,384]{2,1,0:T(8,128)(2,1)S(1)}, bf16[2,2048,384]{2,1,0:T(8,128)(2,1)}, u32[]{:S(2)}) copy-start(bf16[2,2048,384]{2,1,0:T(8,128)(2,1)} %param.12) | copy-start | bytes 9437188
  132.3 3.5 copy-start.5
  188.0 89.5 %all-to-all-start.2 = ((bf16[64,24,2048]{2,1,0:T(8,128)(2,1)}), bf16[64,24,2048]{2,1,0:T(8,128)(2,1)}, u32[]{:S(2)}, u32[]{:S(2)}) async-start(bf16[64,24,2048]{2,1,0:T(8,128)(2,1)} %bitcast.74), calls=%async_computation.2 | async-start | bytes 12582912 | tf_op jit(solution)/shard_map/all_to_all | solution.py:220
  195.5 6.2 %copy-start.12 = (bf16[2,2048,384]{2,1,0:T(8,128)(2,1)S(1)}, bf16[2,2048,384]{2,1,0:T(8,128)(2,1)}, u32[]{:S(2)}) copy-start(bf16[2,2048,384]{2,1,0:T(8,128)(2,1)} %param.12) | copy-start | bytes 9437188
  195.5 6.1 %copy-start.16 = (f32[1536,384]{1,0:T(8,128)S(1)}, f32[1536,384]{1,0:T(8,128)}, u32[]{:S(2)}) copy-start(f32[1536,384]{1,0:T(8,128)} %copy-done.15) | copy-start | bytes 7077892
  195.5 6.1 %copy-start.17 = (f32[1536,384]{1,0:T(8,128)S(1)}, f32[1536,384]{1,0:T(8,128)}, u32[]{:S(2)}) copy-start(f32[1536,384]{1,0:T(8,128)} %get-tuple-element.31) | copy-start | bytes 7077892
  201.6 7.4 %copy-start.14 = (bf16[2,2048,384]{2,1,0:T(8,128)(2,1)S(1)}, bf16[2,2048,384]{2,1,0:T(8,128)(2,1)}, u32[]{:S(2)}) copy-start(bf16[2,2048,384]{2,1,0:T(8,128)(2,1)} %param.10) | copy-start | bytes 9437188
  209.1 13.4 %copy-start.7 = (bf16[1536,384]{1,0:T(8,128)(2,1)}, bf16[1536,384]{1,0:T(8,128)(2,1)S(1)}, u32[]{:S(2)}) copy-start(bf16[1536,384]{1,0:T(8,128)(2,1)S(1)} %get-tuple-element.28) | copy-start | bytes 3538948
  215.8 6.7 %copy-start.10 = (bf16[2,2048,384]{2,1,0:T(8,128)(2,1)S(1)}, bf16[2,2048,384]{2,1,0:T(8,128)(2,1)}, u32[]{:S(2)}) copy-start(bf16[2,2048,384]{2,1,0:T(8,128)(2,1)} %param.11) | copy-start | bytes 9437188
  277.5 89.6 %all-to-all-start.3 = ((bf16[64,24,2048]{2,1,0:T(8,128)(2,1)}), bf16[64,24,2048]{2,1,0:T(8,128)(2,1)}, u32[]{:S(2)}, u32[]{:S(2)}) async-start(bf16[64,24,2048]{2,1,0:T(8,128)(2,1)} %bitcast.75), calls=%async_computation.3 | async-start | bytes 12582912 | tf_op jit(solution)/shard_map/all_to_all | solution.py:220
  285.0 6.7 %copy-start.6 = (bf16[1536,384]{1,0:T(8,128)(2,1)S(1)}, bf16[1536,384]{1,0:T(8,128)(2,1)}, u32[]{:S(2)}) copy-start(bf16[1536,384]{1,0:T(8,128)(2,1)} %copy-done.5) | copy-start | bytes 3538948
  306.4 6.6 %copy-start.8 = (bf16[1536,384]{1,0:T(8,128)(2,1)S(1)}, bf16[1536,384]{1,0:T(8,128)(2,1)}, u32[]{:S(2)}) copy-start(bf16[1536,384]{1,0:T(8,128)(2,1)} %copy-done.7) | copy-start | bytes 3538948
  336.1 38.9 %collective-permute-start.2 = (f32[8,128]{1,0:T(8,128)S(1)}, f32[8,128]{1,0:T(8,128)S(1)}, u32[]{:S(2)}, u32[]{:S(2)}) collective-permute-start(f32[8,128]{1,0:T(8,128)S(1)} %get-tuple-element.27), channel_id=1, source_target_pairs={{0,64},{64,0},{1,65},{65,1},{2,66},{66,2},{3,67},{67,3},{4,68},{68... | collective-permute-start | bytes 12296 | tf_op jit(solution)/shard_map/ppermute | solution.py:224
  339.8 35.8 %collective-permute-start = (bf16[128,1024]{1,0:T(8,128)(2,1)S(1)}, bf16[128,1024]{1,0:T(8,128)(2,1)S(1)}, u32[]{:S(2)}, u32[]{:S(2)}) collective-permute-start(bf16[128,1024]{1,0:T(8,128)(2,1)S(1)} %dynamic-slice_convert_fusion.1), channel_id=1, source_target_pairs={{0,64},{64,0},{1,65},{65,1},{2,66},{66,2},{3,67},{67,3},{4,68},{68... | collective-permute-start | bytes 786440 | tf_op jit(solution)/shard_map/ppermute | solution.py:224
  371.4 10.0 %collective-permute-start.1 = (bf16[128,1024]{1,0:T(8,128)(2,1)S(1)}, bf16[128,1024]{1,0:T(8,128)(2,1)S(1)}, u32[]{:S(2)}, u32[]{:S(2)}) collective-permute-start(bf16[128,1024]{1,0:T(8,128)(2,1)S(1)} %dynamic-slice_convert_fusion), channel_id=1, source_target_pairs={{0,64},{64,0},{1,65},{65,1},{2,66},{66,2},{3,67},{67,3},{4,68},{68... | collective-permute-start | bytes 786440 | tf_op jit(solution)/shard_map/ppermute | solution.py:224
  (1 other events, 0.7 us)
